TPU v7x, 32 devices: a whole 2x2x4 slice. The times are simulated.
32 devices in a mesh: groups: 2 (over y), expert: 16 (over z, x, core), replica: 1.
Axes of the slice: x: 2, y: 2, z: 4, core: 2. Of those that a mesh axis runs over, the one named last changes fastest.
Arguments:
- tokens: bfloat16 [1024, 4096], P(('groups', 'expert'), 'replica'), parts along dimension 0, may hold values from -6 to 6
- down_proj: bfloat16 [4096, 1024], P('replica'), may hold values from -0.09375 to 0.09375
- up_proj: bfloat16 [1024, 4096], P(None, 'replica'), may hold values from -0.1875 to 0.1875
- gate_weight: bfloat16 [16, 1024, 1344], P('expert', None, 'replica'), may hold values from -0.1875 to 0.1875
- lift_weight: bfloat16 [16, 1024, 1344], P('expert', None, 'replica'), may hold values from -0.1875 to 0.1875
- drop_weight: bfloat16 [16, 1344, 1024], P('expert', 'replica'), may hold values from -0.15625 to 0.15625
- routes: int32 [1024, 8], P(('groups', 'expert', 'replica')), parts along dimension 0, may hold values from 0 to 15, all different within a row; in each aligned block of 32 rows (0 to 31, 32 to 63, ...) at most 32 rows name the same one
- route_scale: int32 [1024, 8], P(('groups', 'expert', 'replica')), parts along dimension 0, may hold values from 1 to 16
Outputs:
- mixed: bfloat16 [1024, 4096], P(('groups', 'expert'), 'replica'), parts along dimension 0
There are 2 independent parts, one for each index of `groups`. A program takes and returns all parts, laid end to end along the dimension named above; an argument that names none is the same for every part. Nothing has to cross between parts.
Inputs may be any that keep to these rules, and one draw needn't show every extreme that they name: `routes`: each row names 8 different experts; among the 32 rows of one device, no expert is named by more than 32 of them.
All inputs are finite; a program needn't handle non-finite values.
Results may differ from a plain program's by a relative error of at most 0.015.
Values may be sent and summed in bfloat16 or wider, within the bound.
A program may use at most 64 MiB of HBM per device.

v0:
```python
import jax
import jax.numpy as jnp
from jax import lax
from jax.sharding import PartitionSpec as P


def expert_apply(inputs, gate_weight, lift_weight, drop_weight):
    width = inputs.shape[-1]
    stacked = inputs.reshape(-1, width)
    gate = jnp.dot(stacked, gate_weight[0], preferred_element_type=jnp.float32)
    lifted = jnp.dot(stacked, lift_weight[0], preferred_element_type=jnp.float32)
    hidden = (jax.nn.silu(gate) * lifted).astype(jnp.bfloat16)
    partial_value = jnp.dot(hidden, drop_weight[0], preferred_element_type=jnp.float32)
    return partial_value.reshape(inputs.shape[:-1] + (drop_weight.shape[-1],))


def per_device(
    tokens, down_proj, up_proj, gate_weight, lift_weight, drop_weight, routes, route_scale
):
    paired = lax.axis_size("replica")
    own_rows = tokens.shape[0] // paired
    latent = lax.psum_scatter(
        jnp.dot(tokens, down_proj, preferred_element_type=jnp.float32),
        "replica",
        scatter_dimension=0,
        tiled=True,
    ).astype(jnp.bfloat16)
    width = latent.shape[1]
    experts = gate_weight.shape[0] * lax.axis_size("expert")
    chosen_count = routes.shape[1]
    routed = own_rows * chosen_count
    capacity = min(own_rows, 2 * own_rows * chosen_count // experts)
    flat_routes = routes.reshape(-1)
    onehot = (flat_routes[:, None] == jnp.arange(experts)[None, :]).astype(jnp.float32)
    position = jnp.arange(routed)
    earlier_mask = (position[None, :] < position[:, None]).astype(jnp.float32)
    earlier = jnp.dot(earlier_mask, onehot, precision=lax.Precision.HIGHEST)
    slots = jnp.sum(earlier * onehot, axis=1).astype(jnp.int32)
    target = flat_routes * capacity + slots
    outgoing = jnp.zeros((experts * capacity, width), jnp.bfloat16)
    outgoing = outgoing.at[target].set(latent[position // chosen_count])
    outgoing = outgoing.reshape(experts, capacity, width)
    doubled = jnp.broadcast_to(outgoing[:, None], (experts, paired, capacity, width))
    doubled = doubled.reshape(experts * paired, capacity, width)
    partial_value = expert_apply(
        lax.all_to_all(doubled, ("expert", "replica"), split_axis=0, concat_axis=0, tiled=True),
        gate_weight,
        lift_weight,
        drop_weight,
    )
    partial_value = partial_value.reshape(experts, paired, capacity, width)
    halved = lax.psum_scatter(partial_value, "replica", scatter_dimension=1, tiled=True)
    outcome_local = halved.reshape(experts, capacity, width).astype(jnp.bfloat16)
    returned = lax.all_to_all(outcome_local, "expert", split_axis=0, concat_axis=0, tiled=True)
    picked = returned.reshape(experts * capacity, width)[target]
    scale_f = route_scale.astype(jnp.float32)
    share = scale_f / jnp.sum(scale_f, axis=1, keepdims=True)
    picked = picked.reshape(own_rows, chosen_count, width).astype(jnp.float32)
    combined = jnp.einsum("rk,rkl->rl", share, picked).astype(jnp.bfloat16)
    return jnp.dot(
        lax.all_gather(combined, "replica", axis=0, tiled=True),
        up_proj,
        preferred_element_type=jnp.float32,
    ).astype(jnp.bfloat16)


def solution(mesh):
    in_specs = (
        P(("groups", "expert"), "replica"),
        P("replica", None),
        P(None, "replica"),
        P("expert", None, "replica"),
        P("expert", None, "replica"),
        P("expert", "replica", None),
        P(("groups", "expert", "replica"), None),
        P(("groups", "expert", "replica"), None),
    )
    out_specs = P(("groups", "expert"), "replica")
    return jax.shard_map(
        per_device, mesh=mesh, in_specs=in_specs, out_specs=out_specs, check_vma=False
    )
```

profile of v0, /device:TPU:0, one launch (start us, length us, event | category | flops | bytes accessed | tf_op | source)
XLA Modules:
  0.0 93.2 jit_solution(9743604792299459933)
XLA Ops:
  0.0 0.0 copy-start
  0.0 0.8 broadcast_multiply_fusion
  0.8 0.8 copy.11
  1.6 0.1 copy.10
  1.7 0.1 mul.24
  1.8 0.1 eq.15
  1.9 0.2 fusion.9
  2.1 5.0 %convolution_convert_fusion.1 = bf16[32,1024]{1,0:T(8,128)(2,1)S(1)} fusion(bf16[32,4096]{1,0:T(8,128)(2,1)} %param.8, bf16[4096,1024]{1,0:T(8,128)(2,1)} %param.9), kind=kOutput, calls=%fused_computation.12 | convolution fusion | flops 268468224 | bytes 8716288 | tf_op jit(solution)/shard_map/dot_general | solution.py:23
  7.1 4.5 %scatter_custom_fusion = bf16[512,1024]{1,0:T(8,128)(2,1)} fusion(s32[256]{0:T(256)S(1)} %bitcast.38, bf16[32,1024]{1,0:T(8,128)(2,1)S(1)} %convolution_convert_fusion.1, s32[1024]{0:T(1024)S(1)} %pad_clamp_fusion.1, bf16[]{:T(256)} %constant.22.clone.1), kind=kCustom, calls=%fused_computation.17 | custom fusion | bytes 1048578 | tf_op jit(solution)/shard_map/scatter | solution.py:41
  11.6 32.2 %all_to_all.10 = bf16[16,32,1024]{2,1,0:T(8,128)(2,1)S(1)} all-to-all(bf16[16,32,1024]{2,1,0:T(8,128)(2,1)} %bitcast.34), channel_id=1, replica_groups=mesh['groups'=2,'expert'=16,'replica'=1] {'expert','replica'}, dimensions={0} | all-to-all | bytes 2097152 | tf_op jit(solution)/shard_map/all_to_all | solution.py:46
  43.8 0.0 copy-done
  43.8 0.0 copy-start.2
  43.8 1.6 %fusion.4 = f32[512,1344]{0,1:T(8,128)S(1)} fusion(bf16[512,1024]{1,0:T(8,128)(2,1)S(1)} %bitcast.36, bf16[1,1024,1344]{1,2,0:T(8,128)(2,1)S(1)} %copy-done), kind=kOutput, calls=%fused_computation.9 | convolution fusion | flops 1409286144 | bytes 6553600 | tf_op jit(solution)/shard_map/dot_general | solution.py:10
  45.4 0.1 copy-done.2
  45.6 3.2 %fusion = bf16[512,1344]{0,1:T(8,128)(2,1)} fusion(bf16[512,1024]{1,0:T(8,128)(2,1)S(1)} %bitcast.37, bf16[1,1024,1344]{1,2,0:T(8,128)(2,1)S(1)} %copy-done.2, f32[512,1344]{0,1:T(8,128)S(1)} %fusion.4), kind=kOutput, calls=%fused_computation.5 | convolution fusion | flops 1413414912 | bytes 7929856 | tf_op jit(solution)/shard_map/dot_general | solution.py:11
  48.8 2.5 %copy.12 = bf16[512,1344]{1,0:T(8,128)(2,1)} copy(bf16[512,1344]{0,1:T(8,128)(2,1)} %fusion) | data formatting | bytes 2752512 | tf_op jit(solution)/shard_map/convert_element_type | solution.py:12
  51.3 5.0 %fusion.6 = bf16[16,32,1024]{2,1,0:T(8,128)(2,1)} fusion(bf16[16,32,1344]{2,1,0:T(8,128)(2,1)} %bitcast.35, bf16[1,1344,1024]{2,1,0:T(8,128)(2,1)} %param.13), kind=kOutput, calls=%fused_computation.11 | convolution fusion | flops 1409810432 | bytes 5177344 | tf_op jit(solution)/shard_map/dot_general | solution.py:13
  56.3 5.1 %all-to-all-start.1 = ((bf16[16,32,1024]{2,1,0:T(8,128)(2,1)}), bf16[16,32,1024]{2,1,0:T(8,128)(2,1)}, u32[]{:S(2)}, u32[]{:S(2)}) async-start(bf16[16,32,1024]{2,1,0:T(8,128)(2,1)} %fusion.6), calls=%async_computation.1 | async-start | bytes 2097152 | tf_op jit(solution)/shard_map/all_to_all | solution.py:54
  61.3 0.0 copy-done.1
  61.4 0.1 copy.13
  61.5 22.8 %all-to-all-done.1 = bf16[16,32,1024]{2,1,0:T(8,128)(2,1)} async-done(((bf16[16,32,1024]{2,1,0:T(8,128)(2,1)}), bf16[16,32,1024]{2,1,0:T(8,128)(2,1)}, u32[]{:S(2)}, u32[]{:S(2)}) %all-to-all-start.1) | async-done | bytes 1048608 | tf_op jit(solution)/shard_map/all_to_all | solution.py:54
  84.3 2.9 %gather_fusion = bf16[256,1024]{1,0:T(8,128)(2,1)S(1)} fusion(bf16[512,1024]{1,0:T(8,128)(2,1)} %bitcast.11, s32[1024]{0:T(1024)S(1)} %pad_clamp_fusion), kind=kCustom, calls=%fused_computation.1 | custom fusion | bytes 1049600 | tf_op jit(solution)/shard_map/gather | solution.py:55
  87.3 0.3 fusion.10
  87.5 5.6 %convolution_convert_fusion = bf16[32,4096]{1,0:T(8,128)(2,1)} fusion(bf16[1024,4096]{1,0:T(8,128)(2,1)} %param.10, bf16[32,1,1024]{2,1,0:T(2,128)(2,1)S(1)} %fusion.10), kind=kOutput, calls=%fused_computation.3 | convolution fusion | flops 268566528 | bytes 8716288 | tf_op jit(solution)/shard_map/dot_general | solution.py:60
  (8 shorter events, 0.1 us)
Async XLA Ops:
  0.0 43.8 %copy-start = (bf16[1,1024,1344]{1,2,0:T(8,128)(2,1)S(1)}, bf16[1,1024,1344]{1,2,0:T(8,128)(2,1)}, u32[]{:S(2)}) copy-start(bf16[1,1024,1344]{1,2,0:T(8,128)(2,1)} %param.11) | copy-start | bytes 8257540
  43.8 1.8 %copy-start.2 = (bf16[1,1024,1344]{1,2,0:T(8,128)(2,1)S(1)}, bf16[1,1024,1344]{1,2,0:T(8,128)(2,1)}, u32[]{:S(2)}) copy-start(bf16[1,1024,1344]{1,2,0:T(8,128)(2,1)} %param.12) | copy-start | bytes 8257540
  51.3 10.1 %copy-start.1 = (s32[32,8]{0,1:T(8,128)S(1)}, s32[32,8]{0,1:T(8,128)}, u32[]{:S(2)}) copy-start(s32[32,8]{0,1:T(8,128)} %param.15) | copy-start | bytes 3076
  56.3 28.0 %all-to-all-start.1 = ((bf16[16,32,1024]{2,1,0:T(8,128)(2,1)}), bf16[16,32,1024]{2,1,0:T(8,128)(2,1)}, u32[]{:S(2)}, u32[]{:S(2)}) async-start(bf16[16,32,1024]{2,1,0:T(8,128)(2,1)} %fusion.6), calls=%async_computation.1 | async-start | bytes 2097152 | tf_op jit(solution)/shard_map/all_to_all | solution.py:54
where the time goes:
time: 94.8 us; the launch traced here: 93.2 us
  blocking collectives  32.2 us (34%)
  waiting for transfers between devices  22.8 us (24%)
  matrix products  20.9 us (22%)
  local copies, waits for them, and re-layouts  11.2 us (12%)
  starting transfers between devices  5.06 us (5%)
    all_to_all x1, blocking collectives, per_device(): lax.all_to_all(doubled, ('expert', 'replica'), split_axis=0, concat_axis=...  32.2 us
    all_to_all x1, waiting for transfers between devices, per_device(): lax.all_to_all(outcome_local, 'expert', split_axis=0, concat_axis=0, tile...  22.8 us
    dot_general x1, matrix products, per_device(): jnp.dot(lax.all_gather(combined, 'replica', axis=0, tiled=True), up_proj,...  5.63 us
    all_to_all x1, starting transfers between devices, per_device(): lax.all_to_all(outcome_local, 'expert', split_axis=0, concat_axis=0, tile...  5.06 us
    dot_general x1, matrix products, per_device(): jnp.dot(tokens, down_proj, preferred_element_type=jnp.float32)  5.02 us
    dot_general x1, matrix products, expert_apply(): jnp.dot(hidden, drop_weight[0], preferred_element_type=jnp.float32)  4.98 us
    scatter x1, local copies, waits for them, and re-layouts, per_device(): outgoing = outgoing.at[target].set(latent[position // chosen_count])  4.46 us
    dot_general x1, matrix products, expert_apply(): jnp.dot(stacked, lift_weight[0], preferred_element_type=jnp.float32)  3.18 us
  transfers between devices with their start and end apart: 1, of which 1 were waited for; matrix products, arithmetic and copies ran while one was open for 0% of the time, Pallas kernels for 0%

commit v1 on v0

--- a/solution.py
+++ b/solution.py
@@ -1,7 +1,257 @@
+import functools
+
 import jax
 import jax.numpy as jnp
 from jax import lax
+from jax.experimental import pallas as pl
+from jax.experimental.pallas import tpu as pltpu
 from jax.sharding import PartitionSpec as P
+
+MESH = pl.DeviceIdType.MESH
+LANES = 128
+DOWN_PARTS = 8
+UP_PARTS = 4
+
+
+def flip(value, mask):
+    out, bit = value, 1
+    while bit <= mask:
+        if mask & bit:
+            out = out + bit * (1 - 2 * ((value // bit) % 2))
+        bit *= 2
+    return out
+
+
+def moe_kernel(
+    layers, tokens, down, up, gate, lift, drop, routes, scale, out,
+    tok_v, down_v, up_v, gate_v, lift_v, drop_v, routes_v, scale_v, out_v,
+    lat, part, pair_out, pair_in, side_out, side_in, side_keep, line_out, line_in,
+    load_sem, down_sem, up_sem, out_sem,
+    line_ag_s, line_ag_r, side_ag_s, side_ag_r, pair_ag_s, pair_ag_r,
+    pair_rs_s, pair_rs_r, side_rs_s, side_rs_r, line_rs_s, line_rs_r,
+):
+    me = lax.axis_index("expert")
+    plane, side, core = me // 4, (me // 2) % 2, me % 2
+    rows, width = line_in.shape[1:]
+    depth = tokens.shape[1] // DOWN_PARTS
+    span = out.shape[1] // UP_PARTS
+
+    def at(step, other_side=0, other_core=0):
+        x = 1 - side if other_side else side
+        c = 1 - core if other_core else core
+        return (flip(plane, step) * 2 + x) * 2 + c
+
+    pair_peer, side_peer = at(0, 0, 1), at(0, 1, 0)
+    line_peer = [at(step) for step in range(layers)]
+
+    def send(src, dst, send_sem, recv_sem, peer):
+        return pltpu.make_async_remote_copy(
+            src_ref=src, dst_ref=dst, send_sem=send_sem, recv_sem=recv_sem,
+            device_id={"expert": peer}, device_id_type=MESH,
+        )
+
+    loads = {
+        name: pltpu.make_async_copy(src, dst, load_sem.at[i])
+        for i, (name, src, dst) in enumerate((
+            ("routes", routes, routes_v), ("scale", scale, scale_v), ("tokens", tokens, tok_v),
+            ("gate", gate.at[0], gate_v), ("lift", lift.at[0], lift_v), ("drop", drop.at[0], drop_v),
+        ))
+    }
+    down_loads = [
+        pltpu.make_async_copy(down.at[pl.ds(k * depth, depth)], down_v.at[pl.ds(k * depth, depth)], down_sem.at[k])
+        for k in range(DOWN_PARTS)
+    ]
+    up_loads = [
+        pltpu.make_async_copy(up.at[:, pl.ds(k * span, span)], up_v.at[:, pl.ds(k * span, span)], up_sem.at[k])
+        for k in range(UP_PARTS)
+    ]
+    loads["routes"].start()
+    loads["scale"].start()
+    loads["tokens"].start()
+    for copy in down_loads:
+        copy.start()
+
+    barrier = pltpu.get_barrier_semaphore()
+    peers = [pair_peer, side_peer] + line_peer[1:]
+    for peer in peers:
+        pl.semaphore_signal(barrier, inc=1, device_id={"expert": peer}, device_id_type=MESH)
+
+    loads["routes"].wait()
+    loads["scale"].wait()
+    named, amount = routes_v[...], scale_v[...]
+    lane = lax.broadcasted_iota(jnp.int32, (rows, LANES), 1)
+    dense = jnp.zeros((rows, LANES), jnp.int32)
+    for k in range(named.shape[1]):
+        dense = dense + jnp.where(lane == named[:, k:k + 1], amount[:, k:k + 1], 0)
+    lat[me, :, pl.ds(width, LANES)] = dense.astype(jnp.float32).astype(jnp.bfloat16)
+
+    loads["tokens"].wait()
+    total = jnp.zeros((rows, width), jnp.float32)
+    later = {1: [loads["gate"]], 2: [loads["lift"]], 4: [loads["drop"]], 5: up_loads[:2], 6: up_loads[2:]}
+    for k in range(DOWN_PARTS):
+        down_loads[k].wait()
+        for copy in later.get(k, []):
+            copy.start()
+        total = total + jnp.dot(
+            tok_v[:, k * depth:(k + 1) * depth], down_v[k * depth:(k + 1) * depth, :],
+            preferred_element_type=jnp.float32,
+        )
+    lat[me, :, pl.ds(0, width)] = total.astype(jnp.bfloat16)
+    pl.semaphore_wait(barrier, len(peers))
+
+    sent = []
+
+    def go(copy):
+        copy.start()
+        sent.append(copy)
+
+    def line_ag(step):
+        return send(lat.at[me], lat.at[me], line_ag_s.at[step], line_ag_r.at[step], line_peer[step])
+
+    def side_ag(step):
+        slot = lat.at[at(step)]
+        return send(slot, slot, side_ag_s.at[step], side_ag_r.at[step], side_peer)
+
+    def pair_ag(step, other):
+        slot, i = lat.at[at(step, other)], 2 * step + other
+        return send(slot, slot, pair_ag_s.at[i], pair_ag_r.at[i], pair_peer)
+
+    def got(slot, send_sem, recv_sem):
+        send(lat.at[slot], lat.at[slot], send_sem, recv_sem, pair_peer).wait_recv()
+
+    def from_line(step):
+        got(at(step), line_ag_s.at[step], line_ag_r.at[step])
+        go(side_ag(step))
+        go(pair_ag(step, 0))
+
+    def from_side(step):
+        got(at(step, 1), side_ag_s.at[step], side_ag_r.at[step])
+        go(pair_ag(step, 1))
+
+    def from_pair(step):
+        for other in range(2):
+            i = 2 * step + other
+            got(at(step, other, 1), pair_ag_s.at[i], pair_ag_r.at[i])
+
+    def expert(step):
+        first = flip(plane, step) * 4
+        stacked = lat[pl.ds(first, 4), :, pl.ds(0, width)].reshape(4 * rows, width)
+        gated = jnp.dot(stacked, gate_v[...], preferred_element_type=jnp.float32)
+        lifted = jnp.dot(stacked, lift_v[...], preferred_element_type=jnp.float32)
+        hidden = (gated / (1.0 + jnp.exp(-gated)) * lifted).astype(jnp.bfloat16)
+        value = jnp.dot(hidden, drop_v[...], preferred_element_type=jnp.float32)
+        weights = lat[pl.ds(first, 4), :, pl.ds(width, LANES)].reshape(4 * rows, LANES).astype(jnp.float32)
+        lanes = lax.broadcasted_iota(jnp.int32, weights.shape, 1)
+        mine = jnp.sum(jnp.where(lanes == me, weights, 0.0), axis=1, keepdims=True)
+        part[step] = (value * mine).reshape(4, rows, width)
+        for x in range(2):
+            pair_out[step, x] = part[step, 2 * x + 1 - core].astype(jnp.bfloat16)
+        go(send(pair_out.at[step], pair_in.at[step], pair_rs_s.at[step], pair_rs_r.at[step], pair_peer))
+
+    def to_side(step):
+        send(pair_out.at[step], pair_in.at[step], pair_rs_s.at[step], pair_rs_r.at[step], pair_peer).wait_recv()
+        away = part[step, 2 * (1 - side) + core] + pair_in[step, 1 - side].astype(jnp.float32)
+        side_out[step] = away.astype(jnp.bfloat16)
+        go(send(side_out.at[step], side_in.at[step], side_rs_s.at[step], side_rs_r.at[step], side_peer))
+        side_keep[step] = part[step, 2 * side + core] + pair_in[step, side].astype(jnp.float32)
+
+    def to_line(step):
+        send(side_out.at[step], side_in.at[step], side_rs_s.at[step], side_rs_r.at[step], side_peer).wait_recv()
+        both = side_keep[step] + side_in[step].astype(jnp.float32)
+        if step == 0:
+            side_keep[0] = both
+        else:
+            line_out[step] = both.astype(jnp.bfloat16)
+            go(send(line_out.at[step], line_in.at[step], line_rs_s.at[step], line_rs_r.at[step], line_peer[step]))
+
+    for step in range(layers - 1, 0, -1):
+        go(line_ag(step))
+    go(side_ag(0))
+    go(pair_ag(0, 0))
+    if layers > 1:
+        from_line(1)
+    from_side(0)
+    from_pair(0)
+    loads["gate"].wait()
+    loads["lift"].wait()
+    loads["drop"].wait()
+    for step in range(layers):
+        expert(step)
+        for ahead in (range(2, layers) if step == 0 else ()):
+            from_line(ahead)
+        if step + 1 < layers:
+            from_side(step + 1)
+            from_pair(step + 1)
+        if step >= 1:
+            to_side(step - 1)
+        if step >= 2:
+            to_line(step - 2)
+    to_side(layers - 1)
+    for step in range(max(0, layers - 2), layers):
+        to_line(step)
+
+    gathered = side_keep[0]
+    for step in range(1, layers):
+        send(line_out.at[step], line_in.at[step], line_rs_s.at[step], line_rs_r.at[step], line_peer[step]).wait_recv()
+        gathered = gathered + line_in[step].astype(jnp.float32)
+    whole = jnp.sum(amount.astype(jnp.float32), axis=1, keepdims=True)
+    combined = (gathered / whole).astype(jnp.bfloat16)
+    stores = []
+    for k in range(UP_PARTS):
+        up_loads[k].wait()
+        columns = pl.ds(k * span, span)
+        out_v[:, columns] = jnp.dot(
+            combined, up_v[:, columns], preferred_element_type=jnp.float32
+        ).astype(jnp.bfloat16)
+        copy = pltpu.make_async_copy(out_v.at[:, columns], out.at[:, columns], out_sem.at[k])
+        copy.start()
+        stores.append(copy)
+    for copy in sent:
+        copy.wait_send()
+    for copy in stores:
+        copy.wait()
+
+
+def per_device_line(tokens, down_proj, up_proj, gate_weight, lift_weight, drop_weight, routes, route_scale):
+    experts = lax.axis_size("expert")
+    layers = experts // 4
+    rows, width = tokens.shape[0], down_proj.shape[1]
+    bf16, f32 = jnp.bfloat16, jnp.float32
+    dma = pltpu.SemaphoreType.DMA
+    hbm = pl.BlockSpec(memory_space=pl.ANY)
+    return pl.pallas_call(
+        functools.partial(moe_kernel, layers),
+        out_shape=jax.ShapeDtypeStruct((rows, up_proj.shape[1]), bf16),
+        in_specs=[hbm] * 8,
+        out_specs=hbm,
+        scratch_shapes=[
+            pltpu.VMEM(tokens.shape, bf16),
+            pltpu.VMEM(down_proj.shape, bf16),
+            pltpu.VMEM(up_proj.shape, bf16),
+            pltpu.VMEM(gate_weight.shape[1:], bf16),
+            pltpu.VMEM(lift_weight.shape[1:], bf16),
+            pltpu.VMEM(drop_weight.shape[1:], bf16),
+            pltpu.VMEM(routes.shape, jnp.int32),
+            pltpu.VMEM(route_scale.shape, jnp.int32),
+            pltpu.VMEM((rows, up_proj.shape[1]), bf16),
+            pltpu.VMEM((experts, rows, width + LANES), bf16),
+            pltpu.VMEM((layers, 4, rows, width), f32),
+            pltpu.VMEM((layers, 2, rows, width), bf16),
+            pltpu.VMEM((layers, 2, rows, width), bf16),
+            pltpu.VMEM((layers, rows, width), bf16),
+            pltpu.VMEM((layers, rows, width), bf16),
+            pltpu.VMEM((layers, rows, width), f32),
+            pltpu.VMEM((layers, rows, width), bf16),
+            pltpu.VMEM((layers, rows, width), bf16),
+            dma((6,)), dma((DOWN_PARTS,)), dma((UP_PARTS,)), dma((UP_PARTS,)),
+            dma((layers,)), dma((layers,)), dma((layers,)), dma((layers,)),
+            dma((2 * layers,)), dma((2 * layers,)),
+            dma((layers,)), dma((layers,)), dma((layers,)), dma((layers,)), dma((layers,)), dma((layers,)),
+        ],
+        compiler_params=pltpu.CompilerParams(
+            collective_id=0, has_side_effects=True, vmem_limit_bytes=56 * 1024 * 1024
+        ),
+    )(tokens, down_proj, up_proj, gate_weight, lift_weight, drop_weight, routes, route_scale)
 
 
 def expert_apply(inputs, gate_weight, lift_weight, drop_weight):
@@ -76,6 +326,9 @@
         P(("groups", "expert", "replica"), None),
     )
     out_specs = P(("groups", "expert"), "replica")
+    experts, paired = mesh.shape["expert"], mesh.shape["replica"]
+    layers = experts // 4
+    in_line = paired == 1 and experts == 4 * layers and layers & (layers - 1) == 0
     return jax.shard_map(
-        per_device, mesh=mesh, in_specs=in_specs, out_specs=out_specs, check_vma=False
+        per_device_line if in_line else per_device, mesh=mesh, in_specs=in_specs, out_specs=out_specs, check_vma=False
     )

time: 94.8 us -> 50.8 us (0.54); the launches traced: 93.2 us -> 50.5 us
  Pallas kernels: 0 us -> 38.6 us
  blocking collectives: 32.2 us -> 0 us
  waiting for transfers between devices: 22.8 us -> 0 us
  matrix products: 20.9 us -> 0 us
  starting transfers between devices: 5.06 us -> 0 us
    pallas_call x0 -> x1, Pallas kernels: none -> 38.6 us  [per_device_line(): pl.pallas_call(functools.partial(moe_kernel, layers), out_shape=jax.Shape...]
    all_to_all x1 -> x0, blocking collectives: 32.2 us -> none  [per_device(): lax.all_to_all(doubled, ('expert', 'replica'), split_axis=0, concat_axis=...]
    all_to_all x1 -> x0, waiting for transfers between devices: 22.8 us -> none  [per_device(): lax.all_to_all(outcome_local, 'expert', split_axis=0, concat_axis=0, tile...]
    dot_general x7 -> x0, matrix products: 20.9 us -> none  [the longest x1 5.63 us: per_device(): jnp.dot(lax.all_gather(combined, 'replica', axis=0, tiled=True), up_proj,...]
    unnamed x7, local copies, waits for them, and re-layouts: 0.92 us -> 11.9 us
    all_to_all x1 -> x0, starting transfers between devices: 5.06 us -> none  [per_device(): lax.all_to_all(outcome_local, 'expert', split_axis=0, concat_axis=0, tile...]
    scatter x1 -> x0, local copies, waits for them, and re-layouts: 4.46 us -> none  [per_device(): outgoing = outgoing.at[target].set(latent[position // chosen_count])]
    gather x1 -> x0, local copies, waits for them, and re-layouts: 2.92 us -> none  [per_device(): picked = returned.reshape(experts * capacity, width)[target]]
  transfers between devices with their start and end apart: 1 -> 0, of which waited for: 1 -> 0; matrix products, arithmetic and copies ran while one was open for 0% -> 0% of each run, Pallas kernels for 0% -> 0%
where the time goes in v1:
time: 50.8 us; the launch traced here: 50.5 us
  Pallas kernels  38.6 us (76%)
  local copies, waits for them, and re-layouts  11.9 us (23%)
    pallas_call x1, Pallas kernels, per_device_line(): pl.pallas_call(functools.partial(moe_kernel, layers), out_shape=jax.Shape...  38.6 us
    unnamed x7, local copies, waits for them, and re-layouts  11.9 us

profile of v1, /device:TPU:0, one launch (start us, length us, event | category | flops | bytes accessed | tf_op | source)
XLA Modules:
  0.0 50.5 jit_solution(4643688982706834174)
XLA Ops:
  0.0 0.0 copy-start
  0.0 1.5 %copy.11.routes = s32[32,8]{1,0:T(8,128)} copy(s32[32,8]{0,1:T(8,128)} %param.14) | data formatting | bytes 2048 | tf_op args[6]
  1.5 1.4 %copy.12.scale = s32[32,8]{1,0:T(8,128)} copy(s32[32,8]{0,1:T(8,128)} %param.15) | data formatting | bytes 2048 | tf_op args[7]
  2.9 4.6 %copy.9.gate = bf16[1,1024,1344]{2,1,0:T(8,128)(2,1)} copy(bf16[1,1024,1344]{1,2,0:T(8,128)(2,1)} %param.11) | data formatting | bytes 5505024 | tf_op args[3]
  7.4 0.0 copy-done
  7.4 2.8 %copy.10.lift = bf16[1,1024,1344]{2,1,0:T(8,128)(2,1)} copy(bf16[1,1024,1344]{1,2,0:T(8,128)(2,1)S(1)} %copy-done) | data formatting | bytes 5505024 | tf_op args[4]
  10.3 38.6 %shard_map.82 = bf16[32,4096]{1,0:T(8,128)(2,1)} custom-call(bf16[32,4096]{1,0:T(8,128)(2,1)} %tokens.1, bf16[4096,1024]{1,0:T(8,128)(2,1)} %down.1, bf16[1024,4096]{1,0:T(8,128)(2,1)} %up.1, bf16[1,1024,1344]{2,1,0:T(8,128)(2,1)} %copy.9.gate, bf16[1,1024,1344]{2,1,0:T(8,128)(2,1)} %copy.10.lift, bf16[1,1344,1024]{2,1,0:T(8,128)(2,1)} %drop.1, ...), custom_call_target="tpu_custom_call" | custom-call | tf_op jit(solution)/shard_map/pallas_call | solution.py:222
  48.8 1.7 %copy.14 = bf16[32,4096]{1,0:T(8,128)(2,1)} copy(bf16[32,4096]{1,0:T(8,128)(2,1)} %shard_map.82) | data formatting | bytes 524288
Async XLA Ops:
  0.0 7.4 %copy-start = (bf16[1,1024,1344]{1,2,0:T(8,128)(2,1)S(1)}, bf16[1,1024,1344]{1,2,0:T(8,128)(2,1)}, u32[]{:S(2)}) copy-start(bf16[1,1024,1344]{1,2,0:T(8,128)(2,1)} %param.12) | copy-start | bytes 8257540

commit v2 on v0

--- a/solution.py
+++ b/solution.py
@@ -1,7 +1,319 @@
+import functools
+
 import jax
 import jax.numpy as jnp
 from jax import lax
+from jax.experimental import pallas as pl
+from jax.experimental.pallas import tpu as pltpu
 from jax.sharding import PartitionSpec as P
+
+MESH = pl.DeviceIdType.MESH
+LANES = 128
+DOWN_PARTS = 4
+UP_PARTS = 4
+LAST = (((1,), (1,)), ((), ()))
+
+
+def flip(value, mask):
+    out, bit = value, 1
+    while bit <= mask:
+        if mask & bit:
+            out = out + bit * (1 - 2 * ((value // bit) % 2))
+        bit *= 2
+    return out
+
+
+def moe_kernel(
+    layers, tokens, down, up, gate, lift, drop, routes, scale, out,
+    tok_v, down_v, up_v, gate_v, lift_v, drop_v, routes_v, scale_v, out_v,
+    lat_0, lat_1, part, pair_out, pair_in, side_out, side_in, side_keep, line_out, line_in,
+    load_sem, down_sem, up_sem, out_sem,
+    line_ag_s, line_ag_r, side_ag_s, side_ag_r, pair_ag_s, pair_ag_r,
+    pair_rs_s, pair_rs_r, side_rs_s, side_rs_r, line_rs_s, line_rs_r,
+):
+    me = lax.axis_index("expert")
+    plane, side, core = me // 4, (me // 2) % 2, me % 2
+    rows, half = line_in.shape[2:]
+    depth = tokens.shape[1] // DOWN_PARTS
+    span = out.shape[1] // UP_PARTS
+    lat = (lat_0, lat_1)
+    steps = range(layers)
+
+    def at(step, other_side=0, other_core=0):
+        x = 1 - side if other_side else side
+        c = 1 - core if other_core else core
+        return (flip(plane, step) * 2 + x) * 2 + c
+
+    pair_peer, side_peer = at(0, 0, 1), at(0, 1, 0)
+    line_peer = [at(step) for step in steps]
+
+    def send(src, dst, send_sem, recv_sem, peer):
+        return pltpu.make_async_remote_copy(
+            src_ref=src, dst_ref=dst, send_sem=send_sem, recv_sem=recv_sem,
+            device_id={"expert": peer}, device_id_type=MESH,
+        )
+
+    def columns(q):
+        return pl.ds(q * half, half)
+
+    loads = {
+        name: pltpu.make_async_copy(src, dst, load_sem.at[i])
+        for i, (name, src, dst) in enumerate((
+            ("routes", routes, routes_v), ("scale", scale, scale_v), ("tokens", tokens, tok_v),
+            ("gate", gate.at[0], gate_v), ("lift", lift.at[0], lift_v), ("drop", drop.at[0], drop_v),
+        ))
+    }
+    down_loads = []
+    for q in range(2):
+        for k in range(DOWN_PARTS):
+            block = (pl.ds(k * depth, depth), columns(q))
+            down_loads.append(pltpu.make_async_copy(down.at[block], down_v.at[block], down_sem.at[q, k]))
+    up_loads = [
+        pltpu.make_async_copy(up.at[:, pl.ds(k * span, span)], up_v.at[:, pl.ds(k * span, span)], up_sem.at[k])
+        for k in range(UP_PARTS)
+    ]
+    loads["tokens"].start()
+    for copy in down_loads[:2]:
+        copy.start()
+    loads["routes"].start()
+    loads["scale"].start()
+    for copy in down_loads[2:]:
+        copy.start()
+
+    barrier = pltpu.get_barrier_semaphore()
+    peers = [pair_peer, side_peer] + line_peer[1:]
+    for peer in peers:
+        pl.semaphore_signal(barrier, inc=1, device_id={"expert": peer}, device_id_type=MESH)
+
+    loads["routes"].wait()
+    loads["scale"].wait()
+    named, amount = jnp.transpose(routes_v[...]), jnp.transpose(scale_v[...])
+    lane = lax.broadcasted_iota(jnp.int32, (rows, LANES), 1)
+    dense = jnp.zeros((rows, LANES), jnp.int32)
+    for k in range(named.shape[1]):
+        dense = dense + jnp.where(lane == named[:, k:k + 1], amount[:, k:k + 1], 0)
+    lat_0[me, :, pl.ds(half, LANES)] = dense.astype(jnp.float32).astype(jnp.bfloat16)
+
+    sent = []
+
+    def go(copy):
+        copy.start()
+        sent.append(copy)
+
+    def forward(refs, step, other, q, i, peer):
+        slot = lat[q].at[at(step, other)]
+        go(send(slot, slot, refs[0].at[q, i], refs[1].at[q, i], peer))
+
+    def got(slot, q, recv_sem, i):
+        block = lat[q].at[slot]
+        send(block, block, recv_sem.at[q, i], recv_sem.at[q, i], pair_peer).wait_recv()
+
+    line_ag, side_ag, pair_ag = (line_ag_s, line_ag_r), (side_ag_s, side_ag_r), (pair_ag_s, pair_ag_r)
+
+    def own(q):
+        for step in steps[1:]:
+            block = lat[q].at[me]
+            go(send(block, block, line_ag_s.at[q, step], line_ag_r.at[q, step], line_peer[step]))
+            if step == 1:
+                forward(side_ag, 0, 0, q, 0, side_peer)
+        forward(pair_ag, 0, 0, q, 0, pair_peer)
+
+    def from_line(step, q):
+        got(at(step), q, line_ag_r, step)
+        forward(side_ag, step, 0, q, step, side_peer)
+        forward(pair_ag, step, 0, q, 2 * step, pair_peer)
+
+    def from_side(step, q):
+        got(at(step, 1), q, side_ag_r, step)
+        forward(pair_ag, step, 1, q, 2 * step + 1, pair_peer)
+
+    def from_pair(step):
+        for q in range(2):
+            for other in range(2):
+                got(at(step, other, 1), q, pair_ag_r, 2 * step + other)
+
+    loads["tokens"].wait()
+    later = {
+        (0, 1): [loads["gate"]], (0, 2): [loads["lift"]], (1, 0): [loads["drop"]],
+        (1, 1): up_loads[:2], (1, 2): up_loads[2:],
+    }
+    for q in range(2):
+        total = jnp.zeros((rows, half), jnp.float32)
+        for k in range(DOWN_PARTS):
+            down_loads[q * DOWN_PARTS + k].wait()
+            for copy in later.get((q, k), []):
+                copy.start()
+            total = total + jnp.dot(
+                tok_v[:, k * depth:(k + 1) * depth],
+                down_v[k * depth:(k + 1) * depth, q * half:(q + 1) * half],
+                preferred_element_type=jnp.float32,
+            )
+        lat[q][me, :, pl.ds(0, half)] = total.astype(jnp.bfloat16)
+        if q == 0:
+            pl.semaphore_wait(barrier, len(peers))
+        own(q)
+
+    def inner(step):
+        first = flip(plane, step) * 4
+        stacked = jnp.concatenate(
+            [ref[pl.ds(first, 4), :, pl.ds(0, half)].reshape(4 * rows, half) for ref in lat], axis=1
+        )
+        gated = lax.dot_general(stacked, gate_v[...], LAST, preferred_element_type=jnp.float32)
+        lifted = lax.dot_general(stacked, lift_v[...], LAST, preferred_element_type=jnp.float32)
+        return (gated / (1.0 + jnp.exp(-gated)) * lifted).astype(jnp.bfloat16)
+
+    def outer(step, hidden):
+        first = flip(plane, step) * 4
+        weights = lat_0[pl.ds(first, 4), :, pl.ds(half, LANES)].reshape(4 * rows, LANES).astype(jnp.float32)
+        lanes = lax.broadcasted_iota(jnp.int32, weights.shape, 1)
+        mine = jnp.sum(jnp.where(lanes == me, weights, 0.0), axis=1, keepdims=True)
+        for q in range(2):
+            value = jnp.dot(hidden, drop_v[:, q * half:(q + 1) * half], preferred_element_type=jnp.float32)
+            part[q, step] = (value * mine).reshape(4, rows, half)
+            for x in range(2):
+                pair_out[q, step, x] = part[q, step, 2 * x + 1 - core].astype(jnp.bfloat16)
+            go(pair_rs(step, q))
+
+    def pair_rs(step, q):
+        return send(pair_out.at[q, step], pair_in.at[q, step], pair_rs_s.at[q, step], pair_rs_r.at[q, step], pair_peer)
+
+    def side_rs(step, q):
+        return send(side_out.at[q, step], side_in.at[q, step], side_rs_s.at[q, step], side_rs_r.at[q, step], side_peer)
+
+    def line_rs(step, q):
+        return send(
+            line_out.at[q, step], line_in.at[q, step], line_rs_s.at[q, step], line_rs_r.at[q, step], line_peer[step]
+        )
+
+    def to_side(step, q):
+        pair_rs(step, q).wait_recv()
+        away = part[q, step, 2 * (1 - side) + core] + pair_in[q, step, 1 - side].astype(jnp.float32)
+        side_out[q, step] = away.astype(jnp.bfloat16)
+        go(side_rs(step, q))
+        side_keep[q, step] = part[q, step, 2 * side + core] + pair_in[q, step, side].astype(jnp.float32)
+
+    def to_line(step, q):
+        side_rs(step, q).wait_recv()
+        both = side_keep[q, step] + side_in[q, step].astype(jnp.float32)
+        if step == 0:
+            side_keep[q, 0] = both
+        else:
+            line_out[q, step] = both.astype(jnp.bfloat16)
+            go(line_rs(step, q))
+
+    from_line(1, 0)
+    from_side(0, 0)
+    from_line(2, 0)
+    from_line(3, 0)
+    from_line(1, 1)
+    from_side(0, 1)
+    from_side(1, 0)
+    for name in ("gate", "lift", "drop"):
+        loads[name].wait()
+    from_pair(0)
+    hidden = inner(0)
+    from_line(2, 1)
+    from_line(3, 1)
+    from_side(1, 1)
+    outer(0, hidden)
+    from_side(2, 0)
+    from_pair(1)
+    hidden = inner(1)
+    from_side(3, 0)
+    to_side(0, 0)
+    to_side(0, 1)
+    from_side(2, 1)
+    outer(1, hidden)
+    from_side(3, 1)
+    from_pair(2)
+    hidden = inner(2)
+    to_side(1, 0)
+    to_side(1, 1)
+    outer(2, hidden)
+    to_line(0, 0)
+    to_line(0, 1)
+    from_pair(3)
+    to_line(1, 0)
+    hidden = inner(3)
+    to_side(2, 0)
+    to_side(2, 1)
+    to_line(1, 1)
+    outer(3, hidden)
+    to_line(2, 0)
+    to_side(3, 0)
+    to_line(2, 1)
+    to_side(3, 1)
+    to_line(3, 0)
+    to_line(3, 1)
+
+    whole = jnp.sum(amount.astype(jnp.float32), axis=1, keepdims=True)
+    combined = []
+    for q in range(2):
+        gathered = side_keep[q, 0]
+        for step in steps[1:]:
+            line_rs(step, q).wait_recv()
+            gathered = gathered + line_in[q, step].astype(jnp.float32)
+        combined.append((gathered / whole).astype(jnp.bfloat16))
+    combined = jnp.concatenate(combined, axis=1)
+    stores = []
+    for k in range(UP_PARTS):
+        up_loads[k].wait()
+        block = pl.ds(k * span, span)
+        out_v[:, block] = jnp.dot(
+            combined, up_v[:, block], preferred_element_type=jnp.float32
+        ).astype(jnp.bfloat16)
+        copy = pltpu.make_async_copy(out_v.at[:, block], out.at[:, block], out_sem.at[k])
+        copy.start()
+        stores.append(copy)
+    for copy in sent:
+        copy.wait_send()
+    for copy in stores:
+        copy.wait()
+
+
+def per_device_line(tokens, down_proj, up_proj, gate_weight, lift_weight, drop_weight, routes, route_scale):
+    experts = lax.axis_size("expert")
+    layers = experts // 4
+    rows, half = tokens.shape[0], down_proj.shape[1] // 2
+    bf16, f32 = jnp.bfloat16, jnp.float32
+    gate_weight, lift_weight = jnp.swapaxes(gate_weight, 1, 2), jnp.swapaxes(lift_weight, 1, 2)
+    routes, route_scale = routes.T, route_scale.T
+    dma = pltpu.SemaphoreType.DMA
+    hbm = pl.BlockSpec(memory_space=pl.ANY)
+    return pl.pallas_call(
+        functools.partial(moe_kernel, layers),
+        out_shape=jax.ShapeDtypeStruct((rows, up_proj.shape[1]), bf16),
+        in_specs=[hbm] * 8,
+        out_specs=hbm,
+        scratch_shapes=[
+            pltpu.VMEM(tokens.shape, bf16),
+            pltpu.VMEM(down_proj.shape, bf16),
+            pltpu.VMEM(up_proj.shape, bf16),
+            pltpu.VMEM(gate_weight.shape[1:], bf16),
+            pltpu.VMEM(lift_weight.shape[1:], bf16),
+            pltpu.VMEM(drop_weight.shape[1:], bf16),
+            pltpu.VMEM(routes.shape, jnp.int32),
+            pltpu.VMEM(route_scale.shape, jnp.int32),
+            pltpu.VMEM((rows, up_proj.shape[1]), bf16),
+            pltpu.VMEM((experts, rows, half + LANES), bf16),
+            pltpu.VMEM((experts, rows, half), bf16),
+            pltpu.VMEM((2, layers, 4, rows, half), f32),
+            pltpu.VMEM((2, layers, 2, rows, half), bf16),
+            pltpu.VMEM((2, layers, 2, rows, half), bf16),
+            pltpu.VMEM((2, layers, rows, half), bf16),
+            pltpu.VMEM((2, layers, rows, half), bf16),
+            pltpu.VMEM((2, layers, rows, half), f32),
+            pltpu.VMEM((2, layers, rows, half), bf16),
+            pltpu.VMEM((2, layers, rows, half), bf16),
+            dma((6,)), dma((2, DOWN_PARTS)), dma((UP_PARTS,)), dma((UP_PARTS,)),
+            dma((2, layers)), dma((2, layers)), dma((2, layers)), dma((2, layers)),
+            dma((2, 2 * layers)), dma((2, 2 * layers)),
+            dma((2, layers)), dma((2, layers)), dma((2, layers)), dma((2, layers)), dma((2, layers)), dma((2, layers)),
+        ],
+        compiler_params=pltpu.CompilerParams(
+            collective_id=0, has_side_effects=True, vmem_limit_bytes=56 * 1024 * 1024
+        ),
+    )(tokens, down_proj, up_proj, gate_weight, lift_weight, drop_weight, routes, route_scale)
 
 
 def expert_apply(inputs, gate_weight, lift_weight, drop_weight):
@@ -76,6 +388,8 @@
         P(("groups", "expert", "replica"), None),
     )
     out_specs = P(("groups", "expert"), "replica")
+    experts, paired = mesh.shape["expert"], mesh.shape["replica"]
+    in_line = paired == 1 and experts == 16
     return jax.shard_map(
-        per_device, mesh=mesh, in_specs=in_specs, out_specs=out_specs, check_vma=False
+        per_device_line if in_line else per_device, mesh=mesh, in_specs=in_specs, out_specs=out_specs, check_vma=False
     )

time: 94.8 us -> 42.7 us (0.45); the launches traced: 93.2 us -> 42.5 us
  Pallas kernels: 0 us -> 40.9 us
  blocking collectives: 32.2 us -> 0 us
  waiting for transfers between devices: 22.8 us -> 0 us
  matrix products: 20.9 us -> 0 us
  local copies, waits for them, and re-layouts: 11.2 us -> 1.67 us
  starting transfers between devices: 5.06 us -> 0 us
    pallas_call x0 -> x1, Pallas kernels: none -> 40.9 us  [per_device_line(): pl.pallas_call(functools.partial(moe_kernel, layers), out_shape=jax.Shape...]
    all_to_all x1 -> x0, blocking collectives: 32.2 us -> none  [per_device(): lax.all_to_all(doubled, ('expert', 'replica'), split_axis=0, concat_axis=...]
    all_to_all x1 -> x0, waiting for transfers between devices: 22.8 us -> none  [per_device(): lax.all_to_all(outcome_local, 'expert', split_axis=0, concat_axis=0, tile...]
    dot_general x7 -> x0, matrix products: 20.9 us -> none  [the longest x1 5.63 us: per_device(): jnp.dot(lax.all_gather(combined, 'replica', axis=0, tiled=True), up_proj,...]
    all_to_all x1 -> x0, starting transfers between devices: 5.06 us -> none  [per_device(): lax.all_to_all(outcome_local, 'expert', split_axis=0, concat_axis=0, tile...]
    scatter x1 -> x0, local copies, waits for them, and re-layouts: 4.46 us -> none  [per_device(): outgoing = outgoing.at[target].set(latent[position // chosen_count])]
    gather x1 -> x0, local copies, waits for them, and re-layouts: 2.92 us -> none  [per_device(): picked = returned.reshape(experts * capacity, width)[target]]
    convert_element_type x1 -> x0, local copies, waits for them, and re-layouts: 2.52 us -> none  [expert_apply(): hidden = (jax.nn.silu(gate) * lifted).astype(jnp.bfloat16)]
  transfers between devices with their start and end apart: 1 -> 0, of which waited for: 1 -> 0; matrix products, arithmetic and copies ran while one was open for 0% -> 0% of each run, Pallas kernels for 0% -> 0%
where the time goes in v2:
time: 42.7 us; the launch traced here: 42.5 us
  Pallas kernels  40.9 us (96%)
  local copies, waits for them, and re-layouts  1.67 us (4%)
    pallas_call x1, Pallas kernels, per_device_line(): pl.pallas_call(functools.partial(moe_kernel, layers), out_shape=jax.Shape...  40.9 us
    unnamed x1, local copies, waits for them, and re-layouts  1.67 us

profile of v2, /device:TPU:0, one launch (start us, length us, event | category | flops | bytes accessed | tf_op | source)
XLA Modules:
  0.0 42.5 jit_solution(8121336976225775604)
XLA Ops:
  0.0 40.9 %shard_map.82 = bf16[32,4096]{1,0:T(8,128)(2,1)} custom-call(bf16[32,4096]{1,0:T(8,128)(2,1)} %tokens.1, bf16[4096,1024]{1,0:T(8,128)(2,1)} %down.1, bf16[1024,4096]{1,0:T(8,128)(2,1)} %up.1, bf16[1,1344,1024]{2,1,0:T(8,128)(2,1)} %bitcast.4, bf16[1,1344,1024]{2,1,0:T(8,128)(2,1)} %bitcast.5, bf16[1,1344,1024]{2,1,0:T(8,128)(2,1)} %drop.1, s32[8,32]{1,0:T(8,128)} %bitcast.6, ...), custom_call_target="tpu_custom_call" | custom-call | tf_op jit(solution)/shard_map/pallas_call | solution.py:283
  40.9 1.7 %copy.10 = bf16[32,4096]{1,0:T(8,128)(2,1)} copy(bf16[32,4096]{1,0:T(8,128)(2,1)} %shard_map.82) | data formatting | bytes 524288

commit v3 on v2

--- a/solution.py
+++ b/solution.py
@@ -111,12 +111,16 @@
     line_ag, side_ag, pair_ag = (line_ag_s, line_ag_r), (side_ag_s, side_ag_r), (pair_ag_s, pair_ag_r)
 
     def own(q):
-        for step in steps[1:]:
+        for step in steps[1:3]:
             block = lat[q].at[me]
             go(send(block, block, line_ag_s.at[q, step], line_ag_r.at[q, step], line_peer[step]))
             if step == 1:
                 forward(side_ag, 0, 0, q, 0, side_peer)
         forward(pair_ag, 0, 0, q, 0, pair_peer)
+
+    def far(q):
+        block = lat[q].at[me]
+        go(send(block, block, line_ag_s.at[q, 3], line_ag_r.at[q, 3], line_peer[3]))
 
     def from_line(step, q):
         got(at(step), q, line_ag_r, step)
@@ -202,17 +206,19 @@
             go(line_rs(step, q))
 
     from_line(1, 0)
+    far(0)
     from_side(0, 0)
+    far(1)
     from_line(2, 0)
-    from_line(3, 0)
     from_line(1, 1)
     from_side(0, 1)
     from_side(1, 0)
+    from_line(2, 1)
     for name in ("gate", "lift", "drop"):
         loads[name].wait()
     from_pair(0)
     hidden = inner(0)
-    from_line(2, 1)
+    from_line(3, 0)
     from_line(3, 1)
     from_side(1, 1)
     outer(0, hidden)

time: 42.7 us -> 43 us (level)
  no operation moved by 1% of the time
where the time goes in v3:
time: 43 us; the launch traced here: 42.9 us
  Pallas kernels  41.2 us (96%)
  local copies, waits for them, and re-layouts  1.67 us (4%)
    pallas_call x1, Pallas kernels, per_device_line(): pl.pallas_call(functools.partial(moe_kernel, layers), out_shape=jax.Shape...  41.2 us
    unnamed x1, local copies, waits for them, and re-layouts  1.67 us

profile of v3, /device:TPU:0, one launch (start us, length us, event | category | flops | bytes accessed | tf_op | source)
XLA Modules:
  0.0 42.9 jit_solution(107398100345314393)
XLA Ops:
  0.0 41.2 %shard_map.82 = bf16[32,4096]{1,0:T(8,128)(2,1)} custom-call(bf16[32,4096]{1,0:T(8,128)(2,1)} %tokens.1, bf16[4096,1024]{1,0:T(8,128)(2,1)} %down.1, bf16[1024,4096]{1,0:T(8,128)(2,1)} %up.1, bf16[1,1344,1024]{2,1,0:T(8,128)(2,1)} %bitcast.4, bf16[1,1344,1024]{2,1,0:T(8,128)(2,1)} %bitcast.5, bf16[1,1344,1024]{2,1,0:T(8,128)(2,1)} %drop.1, s32[8,32]{1,0:T(8,128)} %bitcast.6, ...), custom_call_target="tpu_custom_call" | custom-call | tf_op jit(solution)/shard_map/pallas_call | solution.py:289
  41.2 1.7 %copy.10 = bf16[32,4096]{1,0:T(8,128)(2,1)} copy(bf16[32,4096]{1,0:T(8,128)(2,1)} %shard_map.82) | data formatting | bytes 524288
